TPU v7x, 32 devices: a whole 2x2x4 slice. The times are simulated.
32 devices in a mesh: grp: 2 (over x), scen: 16 (over z, y, core).
Axes of the slice: x: 2, y: 2, z: 4, core: 2. Of those that a mesh axis runs over, the one named last changes fastest.
Arguments:
- scenario_rows: bfloat16 [32768, 4096], P(('grp', 'scen')), parts along dimension 0, may hold values from -6 to 6
- row_weights: float32 [32768], P(('grp', 'scen')), parts along dimension 0, may hold values from 0.1 to 10
- row_counts: int32 [32], P(('grp', 'scen')), parts along dimension 0, may hold values from 1 to 1024, 10240 in all
- panel_cols: int32 [1024], P('grp'), parts along dimension 0, may hold values from 0 to 4095, as said below
- regular: float32 [512], replicated, may hold values from 0.2 to 2
- prior_schur: float32 [4096, 4096], P('scen'), as said below
Outputs:
- schur_out: float32 [8192, 4096], P(('grp', 'scen')), parts along dimension 0
- panel_factor: float32 [8192, 512], P(('grp', 'scen')), parts along dimension 0
There are 2 independent parts, one for each index of `grp`. A program takes and returns all parts, laid end to end along the dimension named above; an argument that names none is the same for every part. Nothing has to cross between parts.
Inputs may be any that keep to these rules, and one draw needn't show every extreme that they name: `panel_cols`: the 512 entries are distinct. `row_counts`: the entries of one part along grp sum to 10240. `prior_schur`: symmetric; every eigenvalue is above 0.4, so the regularized block is positive definite.
All inputs are finite; a program needn't handle non-finite values. No bound on the sum of `row_counts` on one device may be relied on, other than what follows from the above.
Results may differ from a plain program's by a relative error of at most 0.0016.
Values sent between devices are 32-bit elements; how exact they have to be, the bound alone decides.
No kernel may reach another device: no remote copies, remote signals or barrier semaphores. Data moves between devices by JAX's collectives and lax.ppermute only.
A program may use at most 128 MiB of HBM per device.

v0:
```python
import jax
import jax.numpy as jnp
from jax import lax
from jax.sharding import PartitionSpec as P


def contract_rows(left, right):
    return lax.dot_general(
        left, right, (((0,), (0,)), ((), ())), preferred_element_type=jnp.float32
    )


def solve_right(lower, values):
    return lax.linalg.triangular_solve(lower, values, left_side=False, lower=True, transpose_a=True)


def shards(scenario_rows, row_weights, row_counts, panel_cols, regular, prior_schur):
    parts = lax.axis_size("scen")
    owned = prior_schur.shape[0]
    depth = scenario_rows.shape[0]
    offset = lax.axis_index("scen") * owned
    live = (jnp.arange(depth, dtype=jnp.int32) < row_counts[0]).astype(jnp.float32)
    factor_w = row_weights * live * (1.0 / (depth * parts))
    picked = jnp.take(scenario_rows, panel_cols, axis=1)
    scaled = (factor_w[:, None] * picked.astype(jnp.float32)).astype(jnp.bfloat16)
    local_cols = jnp.take(prior_schur, panel_cols, axis=1)
    gram_mine = lax.psum_scatter(
        contract_rows(scenario_rows, scaled), "scen", scatter_dimension=0, tiled=True
    )
    panel_rows = gram_mine + local_cols
    select = (panel_cols[:, None] == offset + jnp.arange(owned, dtype=jnp.int32)[None, :]).astype(
        jnp.float32
    )
    block = lax.psum(jnp.dot(select, panel_rows, precision=lax.Precision.HIGHEST), "scen")
    lower = jnp.linalg.cholesky(block + jnp.diag(regular))
    factor_rows = solve_right(lower, panel_rows)
    outer = jnp.dot(
        factor_rows,
        lax.all_gather(factor_rows, "scen", axis=0, tiled=True).T,
        precision=lax.Precision.HIGHEST,
    )
    return (prior_schur - outer, factor_rows)


def solution(mesh):
    placed = (
        P(("grp", "scen"), None),
        P(("grp", "scen")),
        P(("grp", "scen")),
        P("grp"),
        P(),
        P("scen", None),
    )
    return jax.shard_map(
        shards,
        mesh=mesh,
        in_specs=placed,
        out_specs=(P(("grp", "scen"), None), P(("grp", "scen"), None)),
        check_vma=False,
    )
```

profile of v0, /device:TPU:0, one launch (start us, length us, event | category | flops | bytes accessed | tf_op | source)
XLA Modules:
  0.0 480.9 jit_solution(13461781492236821460)
XLA Ops:
  7.2 0.7 compare_and_fusion
  7.9 0.7 compare_select_fusion
  9.3 12.0 %copy.8 = bf16[1024,4096]{0,1:T(8,128)(2,1)} copy(bf16[1024,4096]{1,0:T(8,128)(2,1)} %param.6) | data formatting | bytes 16777216 | tf_op args[0]
  21.2 7.2 %gather_fusion = bf16[512,1024]{1,0:T(8,128)(2,1)S(1)} fusion(bf16[1024,4096]{0,1:T(8,128)(2,1)} %copy.8, s32[1024]{0:T(1024)S(1)} %pad_clamp_fusion), kind=kCustom, calls=%fused_computation | custom fusion | bytes 2099200 | tf_op jit(solution)/shard_map/jit(_take)/gather | solution.py:24
  28.4 10.4 %convolution_bitcast_fusion = f32[4096,512]{0,1:T(8,128)} fusion(bf16[1024,4096]{1,0:T(8,128)(2,1)} %param.6, f32[1024]{0:T(1024)S(1)} %select_multiply_fusion, bf16[512,1024]{1,0:T(8,128)(2,1)S(1)} %gather_fusion, pred[512]{0:T(512)(128)(4,1)S(1)} %compare_and_fusion), kind=kOutput, calls=%fused_computation.4 | convolution fusion | flops 4297064448 | bytes 17830400 | tf_op jit(solution)/shard_map/dot_general | solution.py:8
  38.9 5.6 %copy.9 = f32[256,4096]{0,1:T(8,128)} copy(f32[256,4096]{1,0:T(8,128)} %param.11) | data formatting | bytes 8388608 | tf_op args[5]
  44.5 3.8 gather_fusion.1
  48.3 98.2 %reduce-scatter.2.cloned.1.call-done = f32[256,512]{0,1:T(8,128)} async-done(((f32[4096,512]{0,1:T(8,128)}), f32[256,512]{0,1:T(8,128)}) %reduce-scatter.2.cloned.1.call-update) | async-done | bytes 524304 | tf_op jit(solution)/shard_map/reduce_scatter | solution.py:27
  146.5 1.2 bitcast_add_fusion.1
  147.7 1.7 fusion.5
  149.4 0.2 all-gather.2.cloned.1.call-start
  149.6 94.1 %all-reduce.3.cloned.1.call-done = f32[512,512]{0,1:T(8,128)} async-done(((f32[512,512]{0,1:T(8,128)}), f32[512,512]{0,1:T(8,128)}) %all-reduce.3.cloned.1.call-update) | async-done | bytes 1048592 | tf_op jit(solution)/shard_map/psum | solution.py:34
  243.7 1.3 select_add_fusion
  245.1 0.3 copy.11
  245.4 1.4 fusion
  246.9 11.7 %cholesky.103 = f32[128,128]{1,0:T(8,128)S(1)} custom-call(f32[128,128]{1,0:T(8,128)S(1)} %cholesky.263), custom_call_target="Cholesky" | custom-call | tf_op jit(solution)/shard_map/jit(cholesky)/cholesky | solution.py:35
  258.6 0.1 copy.12
  258.7 9.8 %custom-call.30 = f32[1,128,128]{1,2,0:T(8,128)S(1)} custom-call(f32[1,128,128]{2,1,0:T(8,128)S(1)} %get-tuple-element.31), custom_call_target="InvertDiagBlocksLowerTriangular" | custom-call | tf_op jit(solution)/shard_map/jit(cholesky)/cholesky | solution.py:35
  268.6 0.3 fusion.20
  268.9 0.3 convolution_subtract_fusion.1
  269.2 0.1 copy.13
  269.4 11.7 %cholesky.215 = f32[128,128]{1,0:T(8,128)S(1)} custom-call(f32[128,128]{1,0:T(8,128)S(1)} %cholesky.267), custom_call_target="Cholesky" | custom-call | tf_op jit(solution)/shard_map/jit(cholesky)/cholesky | solution.py:35
  281.1 0.1 copy.14
  281.2 10.0 %custom-call.31 = f32[1,128,128]{1,2,0:T(8,128)S(1)} custom-call(f32[1,128,128]{2,1,0:T(8,128)S(1)} %get-tuple-element.29), custom_call_target="InvertDiagBlocksLowerTriangular" | custom-call | tf_op jit(solution)/shard_map/jit(cholesky)/cholesky | solution.py:35
  291.2 0.1 cholesky.222
  291.4 0.3 convolution_dynamic-update-slice_fusion
  291.7 1.5 convolution_subtract_fusion.4
  293.2 11.7 %cholesky.236 = f32[128,128]{1,0:T(8,128)S(1)} custom-call(f32[128,128]{1,0:T(8,128)S(1)} %cholesky.272), custom_call_target="Cholesky" | custom-call | tf_op jit(solution)/shard_map/jit(cholesky)/cholesky | solution.py:35
  304.9 0.1 copy.16
  305.1 9.8 %custom-call.32 = f32[1,128,128]{1,2,0:T(8,128)S(1)} custom-call(f32[1,128,128]{2,1,0:T(8,128)S(1)} %get-tuple-element.27), custom_call_target="InvertDiagBlocksLowerTriangular" | custom-call | tf_op jit(solution)/shard_map/jit(cholesky)/cholesky | solution.py:35
  314.9 0.3 convolution_dynamic-update-slice_fusion.1
  315.2 1.3 convolution_subtract_fusion.6
  316.5 11.9 %cholesky.253 = f32[128,128]{1,0:T(8,128)S(1)} custom-call(f32[128,128]{1,0:T(8,128)S(1)} %convolution_subtract_fusion.6), custom_call_target="Cholesky" | custom-call | tf_op jit(solution)/shard_map/jit(cholesky)/cholesky | solution.py:35
  328.5 0.1 copy.18
  328.6 0.7 compare_reduce_fusion.1
  329.3 0.6 compare_reduce_fusion
  329.9 0.7 compare_reduce_fusion.2
  333.1 0.1 select_select_fusion
  333.3 8.9 %while.1 = (s32[]{:T(128)}, f32[512,512]{0,1:T(8,128)S(1)}, s32[4,2]{0,1:T(2,128)S(1)}, f32[4,128,128]{2,1,0:T(8,128)S(1)}, s32[]{:T(128)}) while((s32[]{:T(128)}, f32[512,512]{0,1:T(8,128)S(1)}, s32[4,2]{0,1:T(2,128)S(1)}, f32[4,128,128]{2,1,0:T(8,128)S(1)}, s32[]{:T(128)}) %tuple.29), condition=%wide.while_cond, body=%wide.while_body.sunk | while | flops 2 | bytes 393329 | solution.py:14
  333.3 0.1 constant_dynamic-slice_fusion.2
  333.4 0.6 fusion.49
  334.0 1.4 dynamic-slice.7
  335.4 0.1 copy.26
  335.6 0.6 fusion.49
  336.2 1.4 dynamic-slice.7
  337.6 0.1 copy.26
  337.8 0.6 fusion.49
  338.4 1.4 dynamic-slice.7
  339.9 0.1 copy.26
  340.1 0.6 fusion.49
  340.7 1.4 dynamic-slice.7
  342.1 0.1 copy.26
  342.2 39.3 %custom-call.33 = f32[4,128,128]{1,2,0:T(8,128)S(1)} custom-call(f32[4,128,128]{2,1,0:T(8,128)S(1)} %get-tuple-element.9), custom_call_target="InvertDiagBlocksLowerTriangular" | custom-call | tf_op jit(solution)/shard_map/triangular_solve | solution.py:14
  381.6 0.3 fusion.25
  381.9 0.3 convolution_subtract_fusion.5
  382.2 0.3 fusion.29
  382.5 0.4 convolution_subtract_fusion.3
  382.9 0.3 fusion.28
  383.3 0.5 convolution_subtract_fusion.2
  383.8 0.3 fusion.27
  384.1 0.8 pad_maximum_fusion
  384.9 2.0 copy.20
  387.0 75.5 %all-gather.2.cloned.1.call-done = f32[4096,512]{0,1:T(8,128)} async-done(((f32[256,512]{0,1:T(8,128)}), f32[4096,512]{0,1:T(8,128)}) %all-gather.2.cloned.1.call-update) | async-done | bytes 8388624 | tf_op jit(solution)/shard_map/all_gather | solution.py:39
  462.4 11.5 %convolution_subtract_fusion = f32[256,4096]{1,0:T(8,128)} fusion(f32[256,4096]{1,0:T(8,128)} %param.11, f32[4096,512]{0,1:T(8,128)} %all-gather.2.cloned.1.call-done, f32[256,128]{0,1:T(8,128)S(1)} %fusion.27, f32[256,128]{0,1:T(8,128)S(1)} %fusion.28, f32[256,128]{0,1:T(8,128)S(1)} %fusion.29, f32[256,128]{0,1:T(8,128)S(1)} %fusion.25), kind=kOutput, calls=%fused_computation.5 | convolution fusion | flops 6443892736 | bytes 17301504 | tf_op jit(solution)/shard_map/dot_general | solution.py:37
  (37 shorter events, 0.7 us)
Async XLA Ops:
  7.2 139.3 %reduce-scatter.2.cloned.1.call-start = ((), (), s32[]{:S(2)}) async-start(), calls=%async_computation.1 | async-start | bytes 8912896 | tf_op jit(solution)/shard_map/reduce_scatter | solution.py:27
  9.2 12.0 %copy-start.3 = (f32[1024]{0:T(1024)S(1)}, f32[1024]{0:T(1024)}, u32[]{:S(2)}) copy-start(f32[1024]{0:T(1024)} %param.7) | copy-start | bytes 12292
  38.8 108.9 %copy-start.1 = (s32[512]{0:T(512)S(1)}, s32[512]{0:T(512)}, u32[]{:S(2)}) copy-start(s32[512]{0:T(512)} %param.9) | copy-start | bytes 6148
  38.8 204.9 %all-reduce.3.cloned.1.call-start = ((), (), s32[]{:S(2)}) async-start(), calls=%async_computation.2 | async-start | bytes 2097152 | tf_op jit(solution)/shard_map/psum | solution.py:34
  38.9 204.8 %copy-start.2 = (f32[512]{0:T(512)S(1)}, f32[512]{0:T(512)}, u32[]{:S(2)}) copy-start(f32[512]{0:T(512)} %param.10) | copy-start | bytes 6148
  149.4 313.1 %all-gather.2.cloned.1.call-start = ((), (), s32[]{:S(2)}) async-start(), calls=%async_computation.3 | async-start | bytes 8912896 | tf_op jit(solution)/shard_map/all_gather | solution.py:39
  246.9 34.4 %copy-start = (f32[512,512]{1,0:T(8,128)}, f32[512,512]{1,0:T(8,128)S(1)}, u32[]{:S(2)}) copy-start(f32[512,512]{1,0:T(8,128)S(1)} %fusion) | copy-start | bytes 3145732
Sparse Core Ops, SparseCore 0:
  38.9 107.5 reduce-scatter.1
  150.5 93.1 all-reduce.2
  385.1 77.3 all-gather.1
where the time goes:
time: 487 us; the launch traced here: 481 us
  waiting for transfers between devices  268 us (55%)
  other arithmetic  124 us (25%)
  local copies, waits for them, and re-layouts  40.4 us (8%)
  matrix products  30.1 us (6%)
  between operations  17.7 us (4%)
    reduce_scatter x1, waiting for transfers between devices, shards(): lax.psum_scatter(contract_rows(scenario_rows, scaled), 'scen', scatter_di...  98.2 us
    psum x1, waiting for transfers between devices, shards(): lax.psum(jnp.dot(select, panel_rows, precision=lax.Precision.HIGHEST), 's...  94.1 us
    another operation x14, other arithmetic, shards(): lower = jnp.linalg.cholesky(block + jnp.diag(regular))  78.8 us
    all_gather x1, waiting for transfers between devices, shards(): lax.all_gather(factor_rows, 'scen', axis=0, tiled=True)  75.5 us
    another operation x4, other arithmetic, solve_right(): lax.linalg.triangular_solve(lower, values, left_side=False, lower=True, t...  40.3 us
    unnamed x11, local copies, waits for them, and re-layouts  19.6 us
    dot_general x1, matrix products, shards(): jnp.dot(factor_rows, lax.all_gather(factor_rows, 'scen', axis=0, tiled=Tr...  11.5 us
    dot_general x1, matrix products, contract_rows(): lax.dot_general(left, right, (((0,), (0,)), ((), ())), preferred_element_...  10.4 us
  transfers between devices with their start and end apart: 3, of which 3 were waited for; matrix products, arithmetic and copies ran while one was open for 2% of the time, Pallas kernels for 0%

commit v1 on v0

v1 whole, which is shorter than its diff:
```python
import jax
import jax.numpy as jnp
from jax import lax
from jax.experimental import pallas as pl
from jax.experimental.pallas import tpu as pltpu
from jax.sharding import PartitionSpec as P

TILE = 128
GROUP = 8
HIGHEST = lax.Precision.HIGHEST


def contract_rows(left, right):
    return lax.dot_general(
        left, right, (((0,), (0,)), ((), ())), preferred_element_type=jnp.float32
    )


def row_of(values, j):
    return jnp.broadcast_to(values[j : j + 1, :], values.shape)


def invert_tile(rows):
    sub = lax.broadcasted_iota(jnp.int32, (GROUP, TILE), 0)
    lane = lax.broadcasted_iota(jnp.int32, (GROUP, TILE), 1)
    rows = list(rows)
    done = []
    for g in range(len(rows)):
        first = g * GROUP
        in_group = (lane >= first) & (lane < first + GROUP)
        own = rows[g]
        cols = [
            jnp.broadcast_to(own[:, first + k : first + k + 1], own.shape) for k in range(GROUP)
        ]
        recips, pivots, entries = [], jnp.ones_like(own), {}
        for j in range(GROUP):
            pivot = row_of(cols[j], j)
            recip = 1.0 / pivot
            recips.append(recip)
            pivots = jnp.where(sub == j, pivot, pivots)
            mult = jnp.where(sub > j, cols[j] * recip, 0.0)
            for k in range(j + 1, GROUP):
                entries[j, k] = row_of(cols[k], j)
                cols[k] = cols[k] - mult * entries[j, k]
            at = lane == first + j
            own = jnp.where(at & (sub > j), 0.0, own) - mult * jnp.where(at, 1.0, row_of(own, j))
        diag = lane == first + sub
        done.append(
            jnp.where(diag, 1.0, jnp.where(lane < first + sub, own, 0.0)) * lax.rsqrt(pivots)
        )
        spread = []
        for j in range(GROUP):
            row = jnp.where(in_group & (lane > first + j), 0.0, row_of(own, j))
            spread.append(jnp.where(lane == first + j, 1.0, row))
        for h in range(g + 1, len(rows)):
            low = rows[h]
            below = [
                jnp.broadcast_to(low[:, first + k : first + k + 1], low.shape) for k in range(GROUP)
            ]
            low = jnp.where(in_group, 0.0, low)
            for j in range(GROUP):
                mult = below[j] * recips[j]
                for k in range(j + 1, GROUP):
                    below[k] = below[k] - mult * entries[j, k]
                low = low - mult * spread[j]
            rows[h] = low
    return done


def factor_kernel(block_ref, inverse_ref):
    size = block_ref.shape[0]
    tiles = size // TILE
    inverse_ref[...] = block_ref[...]
    row_id = lax.broadcasted_iota(jnp.int32, (TILE, TILE), 0)
    col_id = lax.broadcasted_iota(jnp.int32, (TILE, TILE), 1)
    eye = (row_id == col_id).astype(jnp.float32)

    @pl.loop(0, tiles)
    def _(k):
        at = pl.ds(pl.multiple_of(k * TILE, TILE), TILE)
        tile = inverse_ref[at, at]
        small = jnp.concatenate(
            invert_tile([tile[g * GROUP : (g + 1) * GROUP] for g in range(TILE // GROUP)]), axis=0
        )
        inverse_ref[at, at] = eye
        scaled = jnp.dot(small, inverse_ref[at, :], precision=HIGHEST, preferred_element_type=jnp.float32)
        inverse_ref[at, :] = scaled

        @pl.loop(k + 1, tiles)
        def _(i):
            to = pl.ds(pl.multiple_of(i * TILE, TILE), TILE)
            lower = inverse_ref[at, to]
            inverse_ref[to, at] = jnp.zeros_like(eye)
            inverse_ref[to, :] -= lax.dot_general(
                lower, inverse_ref[at, :], (((0,), (0,)), ((), ())),
                precision=HIGHEST, preferred_element_type=jnp.float32,
            )
            inverse_ref[at, to] = jnp.zeros_like(eye)


def inverse_factor(block):
    size = block.shape[0]
    return pl.pallas_call(
        factor_kernel,
        out_shape=jax.ShapeDtypeStruct(block.shape, jnp.float32),
        in_specs=[pl.BlockSpec(memory_space=pltpu.VMEM)],
        out_specs=pl.BlockSpec(memory_space=pltpu.VMEM),
        cost_estimate=pl.CostEstimate(
            flops=12 * size**3, bytes_accessed=8 * size * size, transcendentals=2 * size
        ),
    )(block)


def shards(scenario_rows, row_weights, row_counts, panel_cols, regular, prior_schur):
    parts = lax.axis_size("scen")
    chips = parts // 2
    owned, order = prior_schur.shape
    depth = scenario_rows.shape[0]
    width = panel_cols.shape[0]
    place = lax.axis_index("scen")
    core = place % 2
    same_core = [list(range(c, parts, 2)) for c in range(2)]
    other_core = [(d, d ^ 1) for d in range(parts)]

    live = (jnp.arange(depth, dtype=jnp.int32) < row_counts[0]).astype(jnp.float32)
    factor_w = row_weights * live * (1.0 / (depth * parts))
    pick = jnp.arange(order, dtype=jnp.int32)[:, None] == panel_cols[None, :]
    picked = jnp.dot(scenario_rows, pick.astype(jnp.bfloat16), preferred_element_type=jnp.float32)
    scaled = (factor_w[:, None] * picked).astype(jnp.bfloat16)
    picked = picked.astype(jnp.bfloat16)

    local_cols = jnp.dot(prior_schur, pick.astype(jnp.float32), precision=HIGHEST)
    select = (panel_cols[:, None] == place * owned + jnp.arange(owned, dtype=jnp.int32)[None, :])
    block = contract_rows(picked, scaled) + jnp.dot(
        select.astype(jnp.float32), local_cols, precision=HIGHEST
    )
    block = 0.5 * (block + block.T)
    block = lax.psum_scatter(block, "scen", scatter_dimension=0, tiled=True)
    block = lax.all_gather(block, "scen", axis=0, tiled=True) + jnp.diag(regular)

    gram = contract_rows(scenario_rows, scaled).reshape(chips, 2, owned, width)
    given = lax.dynamic_index_in_dim(gram, 1 - core, 1, keepdims=False)
    kept = lax.dynamic_index_in_dim(gram, core, 1, keepdims=False)
    both = kept + lax.ppermute(given, "scen", other_core)
    gram_mine = lax.psum_scatter(
        both, "scen", scatter_dimension=0, axis_index_groups=same_core, tiled=False
    )
    panel_rows = gram_mine + local_cols
    panel_half = lax.all_gather(panel_rows, "scen", axis_index_groups=same_core)
    panel_rest = lax.ppermute(panel_half, "scen", other_core)

    inverse = inverse_factor(block)
    factor_rows = jnp.dot(panel_rows, inverse.T, precision=HIGHEST)
    weights = jnp.dot(factor_rows, inverse, precision=HIGHEST)
    even = jnp.where(core == 0, panel_half, panel_rest)
    odd = jnp.where(core == 0, panel_rest, panel_half)
    panel = jnp.stack([even, odd], axis=1).reshape(order, width)
    outer = jnp.dot(weights, panel.T, precision=HIGHEST)
    return (prior_schur - outer, factor_rows)


def solution(mesh):
    placed = (
        P(("grp", "scen"), None),
        P(("grp", "scen")),
        P(("grp", "scen")),
        P("grp"),
        P(),
        P("scen", None),
    )
    return jax.shard_map(
        shards,
        mesh=mesh,
        in_specs=placed,
        out_specs=(P(("grp", "scen"), None), P(("grp", "scen"), None)),
        check_vma=False,
    )
```

time: 487 us -> 333 us (0.68); the launches traced: 481 us -> 332 us
  other arithmetic: 124 us -> 15.4 us
  waiting for transfers between devices: 268 us -> 206 us
  Pallas kernels: 0 us -> 23.4 us
  local copies, waits for them, and re-layouts: 40.4 us -> 31.4 us
  matrix products: 30.1 us -> 37.8 us
    another operation x18 -> x2, other arithmetic: 119 us -> 5.86 us  [shards(): panel = jnp.stack([even, odd], axis=1).reshape(order, width)]
    psum x1 -> x0, waiting for transfers between devices: 94.1 us -> none  [shards(): lax.psum(jnp.dot(select, panel_rows, precision=lax.Precision.HIGHEST), 's...]
    all_gather x1 -> x2, waiting for transfers between devices: 75.5 us -> 112 us  [the longest x1 73.3 us: shards(): panel_half = lax.all_gather(panel_rows, 'scen', axis_index_groups=same_core)]
    pallas_call x0 -> x1, Pallas kernels: none -> 23.4 us  [inverse_factor(): pl.pallas_call(factor_kernel, out_shape=jax.ShapeDtypeStruct(block.shape,...]
    unnamed x11 -> x12, local copies, waits for them, and re-layouts: 19.6 us -> 1.28 us
    dot_general x2 -> x6, matrix products: 13.2 us -> 30.2 us  [the longest x1 8.82 us: shards(): outer = jnp.dot(weights, panel.T, precision=HIGHEST)]
    dynamic_slice x0 -> x2, local copies, waits for them, and re-layouts: none -> 12.7 us  [the longest x1 11.4 us: shards(): kept = lax.dynamic_index_in_dim(gram, core, 1, keepdims=False)]
    reshape x0 -> x1, local copies, waits for them, and re-layouts: none -> 11.7 us  [shards(): gram = contract_rows(scenario_rows, scaled).reshape(chips, 2, owned, width)]
  transfers between devices with their start and end apart: 3 -> 6, of which waited for: 3 -> 5; matrix products, arithmetic and copies ran while one was open for 2% -> 7% of each run, Pallas kernels for 0% -> 7%
where the time goes in v1:
time: 333 us; the launch traced here: 332 us
  waiting for transfers between devices  206 us (62%)
  matrix products  37.8 us (11%)
  local copies, waits for them, and re-layouts  31.4 us (9%)
  Pallas kernels  23.4 us (7%)
  between operations  16.3 us (5%)
  other arithmetic  15.4 us (5%)
    reduce_scatter x1, waiting for transfers between devices, shards(): lax.psum_scatter(both, 'scen', scatter_dimension=0, axis_index_groups=sam...  82.9 us
    all_gather x1, waiting for transfers between devices, shards(): panel_half = lax.all_gather(panel_rows, 'scen', axis_index_groups=same_core)  73.3 us
    all_gather x1, waiting for transfers between devices, shards(): lax.all_gather(block, 'scen', axis=0, tiled=True) + jnp.diag(regular)  39.1 us
    pallas_call x1, Pallas kernels, inverse_factor(): pl.pallas_call(factor_kernel, out_shape=jax.ShapeDtypeStruct(block.shape,...  23.4 us
    reshape x1, local copies, waits for them, and re-layouts, shards(): gram = contract_rows(scenario_rows, scaled).reshape(chips, 2, owned, width)  11.7 us
    dynamic_slice x1, local copies, waits for them, and re-layouts, shards(): kept = lax.dynamic_index_in_dim(gram, core, 1, keepdims=False)  11.4 us
    dot_general x1, matrix products, shards(): outer = jnp.dot(weights, panel.T, precision=HIGHEST)  8.82 us
    dot_general x1, matrix products, shards(): jnp.dot(scenario_rows, pick.astype(jnp.bfloat16), preferred_element_type=...  7.82 us
  transfers between devices with their start and end apart: 6, of which 5 were waited for; matrix products, arithmetic and copies ran while one was open for 7% of the time, Pallas kernels for 7%

profile of v1, /device:TPU:0, one launch (start us, length us, event | category | flops | bytes accessed | tf_op | source)
XLA Modules:
  0.0 331.9 jit_solution(16207682453203480965)
XLA Ops:
  8.0 0.0 reduce-scatter.3.cloned.1.call-start
  8.7 0.7 select_multiply_fusion
  9.4 0.0 copy-start.5
  9.4 7.8 %fusion.3 = f32[512,1024]{1,0:T(8,128)S(1)} fusion(bf16[1024,4096]{1,0:T(8,128)(2,1)} %param.6, s32[512]{0:T(512)} %param.9), kind=kOutput, calls=%fused_computation.5 | convolution fusion | flops 4299161600 | bytes 10487808 | tf_op jit(solution)/shard_map/dot_general | solution.py:128
  17.2 0.0 copy-done.5
  17.2 6.8 %convolution_bitcast_fusion = f32[4096,512]{0,1:T(8,128)} fusion(bf16[1024,4096]{1,0:T(8,128)(2,1)S(1)} %copy-done.5, f32[512,1024]{1,0:T(8,128)S(1)} %fusion.3, f32[1024]{0:T(1024)S(1)} %select_multiply_fusion), kind=kOutput, calls=%fused_computation.3 | convolution fusion | flops 4296015872 | bytes 18878464 | tf_op jit(solution)/shard_map/dot_general | solution.py:14
  24.1 11.7 %reshape.19 = f32[8,2,256,512]{2,1,0,3:T(2,128)} reshape(f32[4096,512]{0,1:T(8,128)} %convolution_bitcast_fusion) | data formatting | bytes 16777216 | tf_op jit(solution)/shard_map/reshape | solution.py:141
  35.8 11.4 %constant_dynamic-slice_fusion.1 = (f32[8,1,256,512]{2,1,0,3:T(1,128)S(1)}, f32[8,1,256,512]{2,1,0,3:T(1,128)S(1)}) fusion(f32[8,2,256,512]{2,1,0,3:T(2,128)} %reshape.19, s32[]{:T(128)S(6)} %select_n.32, s32[]{:T(128)S(6)} %select_n.33), kind=kLoop, calls=%fused_computation.29 | loop fusion | bytes 16777224 | tf_op jit(solution)/shard_map/jit(dynamic_index_in_dim)/dynamic_slice | solution.py:143
  47.2 1.4 copy.27
  48.6 0.5 collective-permute-start
  49.1 6.8 %collective-permute-done = f32[8,256,512]{1,2,0:T(8,128)S(1)} collective-permute-done((f32[8,256,512]{1,2,0:T(8,128)S(1)}, f32[8,256,512]{1,2,0:T(8,128)S(1)}, u32[]{:S(2)}, u32[]{:S(2)}) %collective-permute-start) | collective-permute-done | bytes 4194336 | tf_op jit(solution)/shard_map/ppermute | solution.py:144
  55.9 3.4 %bitcast_add_fusion = f32[8,256,512]{1,2,0:T(8,128)} fusion(f32[8,256,512]{1,2,0:T(8,128)S(1)} %collective-permute-done, f32[8,1,256,512]{2,1,0,3:T(1,128)S(1)} %get-tuple-element.4), kind=kLoop, calls=%fused_computation.7 | loop fusion | flops 1048576 | bytes 12582912 | tf_op jit(solution)/shard_map/add | solution.py:144
  59.2 0.0 copy-start.4
  59.2 0.0 reduce-scatter.3.cloned.1.call-update
  59.3 0.2 all-gather.6.cloned.1.call-start
  59.5 0.4 copy-done.4
  59.9 7.2 %fusion.1 = f32[512,256]{1,0:T(8,128)S(1)} fusion(f32[256,4096]{1,0:T(8,128)} %param.11, s32[512]{0:T(512)S(1)} %copy-done.4), kind=kOutput, calls=%fused_computation.4 | convolution fusion | flops 6446645248 | bytes 4720640 | tf_op jit(solution)/shard_map/dot_general | solution.py:132
  67.2 82.9 %reduce-scatter.3.cloned.1.call-done = f32[1,256,512]{1,2,0:T(8,128)} async-done(((f32[8,256,512]{1,2,0:T(8,128)}), f32[1,256,512]{1,2,0:T(8,128)}) %reduce-scatter.3.cloned.1.call-update) | async-done | bytes 524304 | tf_op jit(solution)/shard_map/reduce_scatter | solution.py:145
  150.1 1.9 bitcast_add_fusion.2
  152.0 0.0 all-gather.6.cloned.1.call-update
  152.0 0.0 reduce-scatter.5.cloned.1.call-start
  152.1 0.7 fusion.8
  152.9 0.7 convolution_add_fusion
  153.6 0.3 copy.17
  153.9 1.2 fusion.7
  155.2 0.0 reduce-scatter.5.cloned.1.call-update
  155.2 0.0 copy-start.3
  155.2 0.3 all-gather.4.cloned.1.call-start
  155.5 73.3 %all-gather.6.cloned.1.call-done = f32[2048,512]{0,1:T(8,128)} async-done(((f32[256,512]{0,1:T(8,128)}), f32[2048,512]{0,1:T(8,128)}) %all-gather.6.cloned.1.call-update) | async-done | bytes 4194320 | tf_op jit(solution)/shard_map/all_gather | solution.py:149
  228.7 5.4 %copy.24 = f32[2048,512]{1,0:T(8,128)} copy(f32[2048,512]{0,1:T(8,128)} %all-gather.6.cloned.1.call-done) | data formatting | bytes 8388608 | tf_op jit(solution)/shard_map/all_gather | solution.py:149
  234.1 0.0 copy-start
  234.1 0.0 collective-permute-start.1
  234.1 4.3 %reduce-scatter.5.cloned.1.call-done = f32[32,512]{1,0:T(8,128)} async-done(((f32[512,512]{1,0:T(8,128)}), f32[32,512]{1,0:T(8,128)}) %reduce-scatter.5.cloned.1.call-update) | async-done | bytes 65552 | tf_op jit(solution)/shard_map/reduce_scatter | solution.py:138
  238.4 0.0 all-gather.4.cloned.1.call-update
  238.5 39.1 %all-gather.4.cloned.1.call-done = f32[512,512]{1,0:T(8,128)} async-done(((f32[32,512]{1,0:T(8,128)}), f32[512,512]{1,0:T(8,128)}) %all-gather.4.cloned.1.call-update) | async-done | bytes 1048592 | tf_op jit(solution)/shard_map/all_gather | solution.py:139
  277.5 0.0 copy-done.3
  277.5 2.4 select_add_fusion.block_ref
  279.9 23.4 %shard_map.77 = f32[512,512]{1,0:T(8,128)} custom-call(f32[512,512]{1,0:T(8,128)} %select_add_fusion.block_ref), custom_call_target="tpu_custom_call" | custom-call | flops 1610612736 | bytes 2097152 | tf_op jit(solution)/shard_map/pallas_call | solution.py:103
  303.3 0.0 copy-done
  303.3 3.1 fusion.13
  306.4 0.0 copy-start.2
  306.4 2.5 fusion.14
  308.9 0.0 collective-permute-done.1
  308.9 4.5 %select_bitcast_fusion.1 = (f32[8,1,256,512]{3,2,1,0:T(8,128)S(1)}, f32[8,1,256,512]{3,2,1,0:T(8,128)S(1)}) fusion(f32[8,256,512]{2,1,0:T(8,128)} %bitcast.39, f32[8,256,512]{2,1,0:T(8,128)} %collective-permute-done.1, pred[]{:T(512)S(6)} %eq.43), kind=kLoop, calls=%fused_computation.10 | loop fusion | flops 2097152 | bytes 16777216 | tf_op jit(solution)/shard_map/stack | solution.py:157
  313.4 0.0 copy-done.2
  313.4 0.0 copy-start.1
  313.5 1.3 pad_maximum_fusion
  314.8 0.8 copy-done.1
  315.6 8.8 %convolution_subtract_fusion = f32[256,4096]{1,0:T(8,128)} fusion(f32[256,4096]{1,0:T(8,128)S(1)} %copy-done.1, f32[256,512]{1,0:T(8,128)S(1)} %fusion.14, f32[4096,512]{1,0:T(8,128)S(1)} %bitcast.37), kind=kOutput, calls=%fused_computation.6 | convolution fusion | flops 6443499520 | bytes 17301504 | tf_op jit(solution)/shard_map/dot_general | solution.py:158
  (1 shorter events, 0.0 us)
Async XLA Ops:
  8.0 142.1 %reduce-scatter.3.cloned.1.call-start = ((), (), s32[]{:S(2)}) async-start(), calls=%async_computation.2 | async-start | bytes 4718592 | tf_op jit(solution)/shard_map/reduce_scatter | solution.py:145
  9.4 7.8 %copy-start.5 = (bf16[1024,4096]{1,0:T(8,128)(2,1)S(1)}, bf16[1024,4096]{1,0:T(8,128)(2,1)}, u32[]{:S(2)}) copy-start(bf16[1024,4096]{1,0:T(8,128)(2,1)} %param.6) | copy-start | bytes 25165828
  48.6 7.3 %collective-permute-start = (f32[8,256,512]{1,2,0:T(8,128)S(1)}, f32[8,256,512]{1,2,0:T(8,128)S(1)}, u32[]{:S(2)}, u32[]{:S(2)}) collective-permute-start(f32[8,256,512]{1,2,0:T(8,128)S(1)} %bitcast.40), channel_id=1, source_target_pairs={{0,1},{1,0},{2,3},{3,2},{4,5},{5,4},{6,7},{7,6},{8,9},{9,8},{10,11... | collective-permute-start | bytes 12582920 | tf_op jit(solution)/shard_map/ppermute | solution.py:144
  59.2 0.7 copy-start.4
  59.3 169.5 %all-gather.6.cloned.1.call-start = ((), (), s32[]{:S(2)}) async-start(), calls=%async_computation.5 | async-start | bytes 4718592 | tf_op jit(solution)/shard_map/all_gather | solution.py:149
  152.0 86.4 %reduce-scatter.5.cloned.1.call-start = ((), (), s32[]{:S(2)}) async-start(), calls=%async_computation.3 | async-start | bytes 1114112 | tf_op jit(solution)/shard_map/reduce_scatter | solution.py:138
  155.2 122.4 %copy-start.3 = (f32[512]{0:T(512)S(1)}, f32[512]{0:T(512)}, u32[]{:S(2)}) copy-start(f32[512]{0:T(512)} %param.10) | copy-start | bytes 6148
  155.2 122.3 %all-gather.4.cloned.1.call-start = ((), (), s32[]{:S(2)}) async-start(), calls=%async_computation.4 | async-start | bytes 1114112 | tf_op jit(solution)/shard_map/all_gather | solution.py:139
  234.1 69.2 %copy-start = (f32[256,512]{0,1:T(8,128)S(1)}, f32[256,512]{0,1:T(8,128)}, u32[]{:S(2)}) copy-start(f32[256,512]{0,1:T(8,128)} %bitcast_add_fusion.2) | copy-start | bytes 1572868
  234.1 74.8 %collective-permute-start.1 = (f32[8,256,512]{2,1,0:T(8,128)}, f32[8,256,512]{2,1,0:T(8,128)}, u32[]{:S(2)}, u32[]{:S(2)}) collective-permute-start(f32[8,256,512]{2,1,0:T(8,128)} %bitcast.38), channel_id=1, source_target_pairs={{0,1},{1,0},{2,3},{3,2},{4,5},{5,4},{6,7},{7,6},{8,9},{9,8},{10,11... | collective-permute-start | bytes 12582920 | tf_op jit(solution)/shard_map/ppermute | solution.py:150
  306.4 7.0 %copy-start.2 = (f32[256,512]{1,0:T(8,128)}, f32[256,512]{1,0:T(8,128)S(1)}, u32[]{:S(2)}) copy-start(f32[256,512]{1,0:T(8,128)S(1)} %fusion.13) | copy-start | bytes 1572868
  313.4 2.2 copy-start.1
Sparse Core Ops, SparseCore 0:
  59.4 90.6 reduce-scatter.2
  152.7 75.9 all-gather.5
Sparse Core Ops, SparseCore 1:
  156.6 81.8 reduce-scatter.4
  240.5 37.0 all-gather.3
